TPU v7x, 128 devices: a whole 4x4x4 slice. The times are simulated.
128 devices in a mesh: seq: 128 (over y, x, z, core).
Axes of the slice: x: 4, y: 4, z: 4, core: 2. Of those that a mesh axis runs over, the one named last changes fastest.
Arguments:
- tokens: bfloat16 [32768, 640], P('seq'), may hold values from -6 to 6
- starts: int32 [128], replicated, may hold values from 0 to 1, as said below
- query_weight: bfloat16 [640, 1024], P('seq'), may hold values from -0.25 to 0.25
- key_weight: bfloat16 [640, 256], P('seq'), may hold values from -0.25 to 0.25
- value_weight: bfloat16 [640, 256], P('seq'), may hold values from -0.25 to 0.25
- output_weight: bfloat16 [1024, 640], P('seq'), may hold values from -0.1875 to 0.1875
- gate_weight: bfloat16 [640, 2048], P('seq'), may hold values from -0.25 to 0.25
- up_weight: bfloat16 [640, 2048], P('seq'), may hold values from -0.25 to 0.25
- down_weight: bfloat16 [2048, 640], P('seq'), may hold values from -0.125 to 0.125
- input_gain: float32 [640], replicated, may hold values from 0.25 to 1.75
- query_gain: float32 [256], replicated, may hold values from 0.25 to 1.75
- key_gain: float32 [256], replicated, may hold values from 0.25 to 1.75
- attn_gain: float32 [640], replicated, may hold values from 0.25 to 1.75
- ffn_gain: float32 [640], replicated, may hold values from 0.25 to 1.75
- ffn_out_gain: float32 [640], replicated, may hold values from 0.25 to 1.75
- cotangent: bfloat16 [32768, 640], P('seq'), may hold values from -6 to 6
Outputs:
- output: bfloat16 [32768, 640], P('seq')
- input_grad: bfloat16 [32768, 640], P('seq')
- grad_query_weight: float32 [640, 1024], P('seq')
- grad_key_weight: float32 [640, 256], P('seq')
- grad_value_weight: float32 [640, 256], P('seq')
- grad_output_weight: float32 [1024, 640], P('seq')
- grad_gate_weight: float32 [640, 2048], P('seq')
- grad_up_weight: float32 [640, 2048], P('seq')
- grad_down_weight: float32 [2048, 640], P('seq')
- grad_input_gain: float32 [640], replicated
- grad_query_gain: float32 [256], replicated
- grad_key_gain: float32 [256], replicated
- grad_attn_gain: float32 [640], replicated
- grad_ffn_gain: float32 [640], replicated
- grad_ffn_out_gain: float32 [640], replicated
Inputs may be any that keep to these rules, and one draw needn't show every extreme that they name: starts[0] is 1; a sequence runs from a group with starts 1 up to the next such group; every sequence but the last holds between max(1, 8) and max(1, 32) groups, the last ends with the array.
All inputs are finite; a program needn't handle non-finite values.
Results may differ from a plain program's by a relative error of at most 0.019.
Values may be sent and summed in bfloat16 or wider, within the bound.
No kernel may reach another device: no remote copies, remote signals or barrier semaphores. Data moves between devices by JAX's collectives and lax.ppermute only.
A program may use at most 128 MiB of HBM per device.

v0:
```python
from functools import partial
import math

import jax
import jax.numpy as jnp
from jax import lax
from jax.sharding import PartitionSpec as P

WINDOW = 512


norm_epsilon = 1e-06
rope_base = 10000.0


def shifted(value, axis, steps):
    count = lax.axis_size(axis)
    leading, last = (max(0, -steps), min(count, count - steps))
    return lax.ppermute(value, axis, [(source, source + steps) for source in range(leading, last)])


def shortened(shard):
    return jax.tree.map(lambda a: a.astype(jnp.bfloat16) if a.dtype == jnp.float32 else a, shard)


def rms_scale(values, gain):
    mean_square = jnp.mean(values * values, axis=-1, keepdims=True)
    return values * lax.rsqrt(mean_square + norm_epsilon) * gain


def rope_tables(position, head_dim):
    half = head_dim // 2
    exponent = jnp.arange(half, dtype=jnp.float32) * (2.0 / head_dim)
    inverse = jnp.power(jnp.float32(rope_base), -exponent)
    angles = position.astype(jnp.float32)[:, None] * inverse[None, :]
    return (jnp.cos(angles)[:, None, :], jnp.sin(angles)[:, None, :])


def head_prep(pre, gain, cosine, sine):
    normed = rms_scale(pre, gain)
    half = normed.shape[-1] // 2
    first = normed[..., :half]
    second = normed[..., half:]
    return jnp.concatenate(
        [first * cosine - second * sine, second * cosine + first * sine], axis=-1
    )


def gated(gate, upward):
    return jax.nn.gelu(gate, approximate=True) * upward


def product(left, right):
    return jnp.dot(left, right, preferred_element_type=jnp.float32)


def transposed_left(left, right):
    return lax.dot_general(
        left, right, (((0,), (0,)), ((), ())), preferred_element_type=jnp.float32
    )


def transposed_right(left, right):
    return lax.dot_general(
        left, right, (((1,), (1,)), ((), ())), preferred_element_type=jnp.float32
    )


def body(
    tokens,
    starts,
    query_weight,
    key_weight,
    value_weight,
    output_weight,
    gate_weight,
    up_weight,
    down_weight,
    input_gain,
    query_gain,
    key_gain,
    attn_gain,
    ffn_gain,
    ffn_out_gain,
    cotangent,
):
    span = tokens.shape[0]
    head_dim = key_weight.shape[1]
    heads = query_weight.shape[1] // head_dim
    hops = max(1, WINDOW // span)
    halo = min(span, WINDOW)
    extent = hops * halo + span
    scale = 1.0 / math.sqrt(head_dim)
    gathered = (
        lax.all_gather(query_weight, "seq", axis=0, tiled=True),
        lax.all_gather(key_weight, "seq", axis=0, tiled=True),
        lax.all_gather(value_weight, "seq", axis=0, tiled=True),
        lax.all_gather(output_weight, "seq", axis=0, tiled=True),
        lax.all_gather(gate_weight, "seq", axis=0, tiled=True),
        lax.all_gather(up_weight, "seq", axis=0, tiled=True),
        lax.all_gather(down_weight, "seq", axis=0, tiled=True),
    )
    full_query, full_key, full_value, full_output, full_gate, full_up, full_down = gathered
    group = lax.axis_index("seq")
    group_ids = jnp.arange(starts.shape[0], dtype=jnp.int32)
    first_group = jnp.max(jnp.where((group_ids <= group) & (starts == 1), group_ids, 0))
    seq_first = first_group * span
    query_global = group * span + jnp.arange(span, dtype=jnp.int32)
    position = query_global - seq_first
    x_float = tokens.astype(jnp.float32)
    normed_in = rms_scale(x_float, input_gain).astype(jnp.bfloat16)
    query_pre = product(normed_in, full_query).reshape(span, heads, head_dim)
    key_pre = product(normed_in, full_key).reshape(span, 1, head_dim)
    value_bf = product(normed_in, full_value).astype(jnp.bfloat16)
    cosine, sine = rope_tables(position, head_dim)
    prepare = partial(head_prep, cosine=cosine, sine=sine)
    query_bf = prepare(query_pre, query_gain).astype(jnp.bfloat16)
    key_bf = prepare(key_pre, key_gain).astype(jnp.bfloat16).reshape(span, head_dim)
    tails = (key_bf, value_bf)
    received = []
    piece = tails
    for step in range(hops):
        piece = shifted((piece[0], piece[1]), "seq", 1)
        received.append(piece)
    keys_all = jnp.concatenate(
        [received[hops - 1 - order][0] for order in range(hops)] + [key_bf], axis=0
    )
    values_all = jnp.concatenate(
        [received[hops - 1 - order][1] for order in range(hops)] + [value_bf], axis=0
    )
    key_global = group * span - hops * halo + jnp.arange(extent, dtype=jnp.int32)
    offset = query_global[:, None] - key_global[None, :]
    valid = (offset >= 0) & (offset < WINDOW) & (key_global[None, :] >= seq_first)
    query_flat = query_bf.reshape(span * heads, head_dim)
    scores = (transposed_right(query_flat, keys_all) * scale).reshape(span, heads, extent)
    scores = jnp.where(valid[:, None, :], scores, -1e30)
    peak = jnp.max(scores, axis=-1, keepdims=True)
    log_total = peak + jnp.log(jnp.sum(jnp.exp(scores - peak), axis=-1, keepdims=True))
    probs = jnp.exp(scores - log_total).reshape(span * heads, extent)
    probs_bf = probs.astype(jnp.bfloat16)
    attended_bf = product(probs_bf, values_all).reshape(span, heads * head_dim).astype(jnp.bfloat16)
    projected = product(attended_bf, full_output)
    resid = x_float + rms_scale(projected, attn_gain)
    normed_ffn = rms_scale(resid, ffn_gain).astype(jnp.bfloat16)
    gate = product(normed_ffn, full_gate)
    upward = product(normed_ffn, full_up)
    mixed_bf = gated(gate, upward).astype(jnp.bfloat16)
    down = product(mixed_bf, full_down)
    output = resid + rms_scale(down, ffn_out_gain)
    back_query, back_key, back_value = (full_query, full_key, full_value)
    back_output, back_gate, back_up, back_down = (full_output, full_gate, full_up, full_down)
    out_grad = cotangent.astype(jnp.float32)
    d_down, grad_ffn_out = jax.vjp(rms_scale, down, ffn_out_gain)[1](out_grad)
    d_down_bf = d_down.astype(jnp.bfloat16)
    grad_down = transposed_left(mixed_bf, d_down_bf)
    d_mixed = transposed_right(d_down_bf, back_down)
    d_gate, d_upward = jax.vjp(gated, gate, upward)[1](d_mixed)
    d_gate_bf = d_gate.astype(jnp.bfloat16)
    d_upward_bf = d_upward.astype(jnp.bfloat16)
    grad_gate = transposed_left(normed_ffn, d_gate_bf)
    grad_up = transposed_left(normed_ffn, d_upward_bf)
    d_normed_ffn = transposed_right(d_gate_bf, back_gate) + transposed_right(d_upward_bf, back_up)
    d_resid_part, grad_ffn = jax.vjp(rms_scale, resid, ffn_gain)[1](d_normed_ffn)
    d_resid = out_grad + d_resid_part
    d_projected, grad_attn = jax.vjp(rms_scale, projected, attn_gain)[1](d_resid)
    d_projected_bf = d_projected.astype(jnp.bfloat16)
    grad_output = transposed_left(attended_bf, d_projected_bf)
    d_attended_bf = transposed_right(d_projected_bf, back_output).astype(jnp.bfloat16)
    d_attended_bf = d_attended_bf.reshape(span * heads, head_dim)
    d_probs = transposed_right(d_attended_bf, values_all)
    balance = jnp.sum(d_probs * probs, axis=-1, keepdims=True)
    d_scores_bf = (probs * (d_probs - balance)).astype(jnp.bfloat16)
    d_query_bf = (
        (product(d_scores_bf, keys_all) * scale).astype(jnp.bfloat16).reshape(span, heads, head_dim)
    )
    d_keys_all = transposed_left(d_scores_bf, query_flat) * scale
    d_values_all = transposed_left(probs_bf, d_attended_bf)
    carry = None
    for step in range(hops, 0, -1):
        begin = (hops - step) * halo
        part = (d_keys_all[begin : begin + halo], d_values_all[begin : begin + halo])
        if carry is not None:
            part = (carry[0] + part[0], carry[1] + part[1])
        carry = shifted((shortened(part[0]), shortened(part[1])), "seq", -1)
    back_keys, back_values = carry
    own_keys = d_keys_all[hops * halo :]
    own_values = d_values_all[hops * halo :]
    d_key = jnp.concatenate([own_keys[: span - halo], own_keys + back_keys], axis=0)
    d_value_bf = jnp.concatenate(
        [own_values[: span - halo], own_values + back_values], axis=0
    ).astype(jnp.bfloat16)
    d_key_bf = d_key.astype(jnp.bfloat16)
    d_key_pre, grad_key_gain = jax.vjp(prepare, key_pre, key_gain)[1](
        d_key_bf.astype(jnp.float32).reshape(span, 1, head_dim)
    )
    d_key_pre_bf = d_key_pre.reshape(span, head_dim).astype(jnp.bfloat16)
    d_query_pre, grad_query_gain = jax.vjp(prepare, query_pre, query_gain)[1](
        d_query_bf.astype(jnp.float32)
    )
    d_query_pre_bf = d_query_pre.reshape(span, heads * head_dim).astype(jnp.bfloat16)
    grad_query = transposed_left(normed_in, d_query_pre_bf)
    grad_key = transposed_left(normed_in, d_key_pre_bf)
    grad_value = transposed_left(normed_in, d_value_bf)
    d_normed_in = (
        transposed_right(d_query_pre_bf, back_query)
        + transposed_right(d_key_pre_bf, back_key)
        + transposed_right(d_value_bf, back_value)
    )
    d_input_part, grad_input = jax.vjp(rms_scale, x_float, input_gain)[1](d_normed_in)
    input_grad = (d_resid + d_input_part).astype(jnp.bfloat16)
    summed = (
        lax.psum_scatter(grad_query, "seq", scatter_dimension=0, tiled=True),
        lax.psum_scatter(grad_key, "seq", scatter_dimension=0, tiled=True),
        lax.psum_scatter(grad_value, "seq", scatter_dimension=0, tiled=True),
        lax.psum_scatter(grad_output, "seq", scatter_dimension=0, tiled=True),
        lax.psum_scatter(grad_gate, "seq", scatter_dimension=0, tiled=True),
        lax.psum_scatter(grad_up, "seq", scatter_dimension=0, tiled=True),
        lax.psum_scatter(grad_down, "seq", scatter_dimension=0, tiled=True),
    )
    gains = lax.psum(
        (grad_input, grad_query_gain, grad_key_gain, grad_attn, grad_ffn, grad_ffn_out), "seq"
    )
    return (
        output.astype(jnp.bfloat16),
        input_grad,
        summed[0],
        summed[1],
        summed[2],
        summed[3],
        summed[4],
        summed[5],
        summed[6],
        gains[0],
        gains[1],
        gains[2],
        gains[3],
        gains[4],
        gains[5],
    )


def solution(mesh):
    return jax.shard_map(
        body,
        mesh=mesh,
        in_specs=(
            P("seq", None),
            P(),
            P("seq", None),
            P("seq", None),
            P("seq", None),
            P("seq", None),
            P("seq", None),
            P("seq", None),
            P("seq", None),
            P(),
            P(),
            P(),
            P(),
            P(),
            P(),
            P("seq", None),
        ),
        out_specs=(
            P("seq", None),
            P("seq", None),
            P("seq", None),
            P("seq", None),
            P("seq", None),
            P("seq", None),
            P("seq", None),
            P("seq", None),
            P("seq", None),
            P(),
            P(),
            P(),
            P(),
            P(),
            P(),
        ),
        check_vma=False,
    )
```

profile of v0, /device:TPU:0, one launch (start us, length us, event | category | flops | bytes accessed | tf_op | source)
XLA Modules:
  0.0 1276.5 jit_solution(10282654226571809464)
XLA Ops:
  12.0 38.2 %all-gather.1 = bf16[128,5,256]{2,1,0:T(8,128)(2,1)S(1)} all-gather(bf16[1,5,256]{2,1,0:T(8,128)(2,1)} %bitcast.82), channel_id=1, replica_groups=mesh['seq'=128] {'seq'}, dimensions={0}, use_global_device_ids=true | all-gather | bytes 330240 | tf_op jit(solution)/shard_map/all_gather | solution.py:96
  51.7 1.4 multiply_reduce_fusion.11
  54.6 2.3 collective-permute-start
  56.9 34.0 %all-gather.2 = bf16[128,5,256]{2,1,0:T(8,128)(2,1)S(1)} all-gather(bf16[1,5,256]{2,1,0:T(8,128)(2,1)S(1)} %bitcast.83), channel_id=1, replica_groups=mesh['seq'=128] {'seq'}, dimensions={0}, use_global_device_ids=true | all-gather | bytes 330240 | tf_op jit(solution)/shard_map/all_gather | solution.py:97
  91.4 2.9 collective-permute-start.2
  96.1 1.8 copy.42
  98.4 2.1 collective-permute-start.1
  100.5 3.0 collective-permute-start.3
  103.6 2.6 reshape.402
  110.6 1.7 fusion.82
  113.2 2.4 convolution_convert_fusion.1
  115.6 2.2 convert_element_type.118
  117.8 25.4 %all-gather.11.cloned.1.call-done = bf16[1024,640]{1,0:T(8,128)(2,1)} async-done(((bf16[8,640]{1,0:T(8,128)(2,1)}), bf16[1024,640]{1,0:T(8,128)(2,1)}) %all-gather.11.cloned.1.call-update) | async-done | bytes 1310736 | tf_op jit(solution)/shard_map/all_gather | solution.py:98
  143.2 2.1 multiply_reduce_fusion.10
  148.4 62.4 %all-gather.17.cloned.1.call-done = bf16[128,5,2048]{2,1,0:T(8,128)(2,1)} async-done(((bf16[1,5,2048]{2,1,0:T(8,128)(2,1)}), bf16[128,5,2048]{2,1,0:T(8,128)(2,1)}) %all-gather.17.cloned.1.call-update) | async-done | bytes 2621456 | tf_op jit(solution)/shard_map/all_gather | solution.py:99
  210.8 5.6 reshape.408
  216.4 61.8 %all-gather.19.cloned.1.call-done = bf16[128,5,2048]{2,1,0:T(8,128)(2,1)} async-done(((bf16[1,5,2048]{2,1,0:T(8,128)(2,1)}), bf16[128,5,2048]{2,1,0:T(8,128)(2,1)}) %all-gather.19.cloned.1.call-update) | async-done | bytes 2621456 | tf_op jit(solution)/shard_map/all_gather | solution.py:100
  278.2 5.6 reshape.410
  283.9 3.0 fusion.83
  286.8 1.3 copy-done.26
  288.2 2.9 multiply_convert_fusion.2
  291.1 53.1 %all-gather.13.cloned.1.call-done = bf16[2048,640]{1,0:T(8,128)(2,1)} async-done(((bf16[16,640]{1,0:T(8,128)(2,1)}), bf16[2048,640]{1,0:T(8,128)(2,1)}) %all-gather.13.cloned.1.call-update) | async-done | bytes 2621456 | tf_op jit(solution)/shard_map/all_gather | solution.py:101
  344.2 3.3 multiply_reduce_fusion.8
  349.4 2.5 multiply_convert_fusion.1
  353.0 3.2 fusion.87
  356.2 3.3 fusion.88
  359.6 1.8 multiply_reduce_fusion.4
  364.1 1.4 convolution_convert_fusion
  365.5 2.2 reshape.394
  367.7 2.6 fusion.27
  370.3 1.7 multiply_reduce_fusion
  376.6 1.3 multiply_add_fusion.1
  380.0 1.4 collective-permute-start.6
  381.5 2.1 fusion.75
  383.7 2.1 fusion.86
  388.1 1.5 collective-permute-start.7
  389.6 1.6 collective-permute-done.5
  396.0 3.4 fusion.89
  401.4 1.4 fusion.18
  402.8 72.5 %all-reduce.10 = (f32[640]{0:T(1024)}, f32[256]{0:T(256)}, f32[256]{0:T(256)}, f32[640]{0:T(1024)}, f32[640]{0:T(1024)}, /*index=5*/f32[640]{0:T(1024)}) all-reduce(f32[640]{0:T(1024)S(1)} %get-tuple-element.23, f32[256]{0:T(256)S(1)} %get-tuple-element.15, f32[256]{0:T(256)S(1)} %get-tuple-element.25, ...), channel_id=1, replica_groups=mesh['seq'=128] {'seq'}, use_global_device_ids=true, to_apply=%region_24.25 | all-reduce | flops 3072 | bytes 24576 | tf_op jit(solution)/shard_map/psum | solution.py:220
  476.3 146.1 %all-reduce.14.cloned.1.call-done = (f32[640,1024]{1,0:T(8,128)}, f32[640,256]{1,0:T(8,128)}, f32[640,256]{1,0:T(8,128)}, f32[1024,640]{1,0:T(8,128)}, f32[640,2048]{1,0:T(8,128)}, /*index=5*/f32[640,2048]{1,0:T(8,128)}) async-done(((f32[640,1024]{1,0:T(8,128)}, f32[640,256]{1,0:T(8,128)}, f32[640,256]{1,0:T(8,128)}, f32[1024,640]{1,0:T(8,128)}, f32[640,2048]{1,0:T(8,128)}, ...) | async-done | bytes 17039376
  622.4 1.3 constant_dynamic-slice_fusion.4
  623.8 1.3 constant_dynamic-slice_fusion.3
  625.1 1.3 constant_dynamic-slice_fusion.2
  626.4 1.5 constant_dynamic-slice_fusion.5
  627.9 1.5 constant_dynamic-slice_fusion.1
  629.4 1.5 constant_dynamic-slice_fusion
  631.0 638.2 %reduce-scatter.2.cloned.1.call-done = f32[16,640]{1,0:T(8,128)} async-done(((f32[2048,640]{1,0:T(8,128)}), f32[16,640]{1,0:T(8,128)}) %reduce-scatter.2.cloned.1.call-update) | async-done | bytes 40976 | tf_op jit(solution)/shard_map/reduce_scatter | solution.py:218
  (273 shorter events, 40.0 us)
Async XLA Ops:
  7.2 46.7 %copy-start.72 = (f32[256]{0:T(256)S(1)}, f32[256]{0:T(256)}, u32[]{:S(2)}) copy-start(f32[256]{0:T(256)} %param.27) | copy-start | bytes 3076
  7.2 49.7 %copy-start.82 = (bf16[5,256]{1,0:T(8,128)(2,1)S(1)}, bf16[5,256]{1,0:T(8,128)(2,1)}, u32[]{:S(2)}) copy-start(bf16[5,256]{1,0:T(8,128)(2,1)} %param.20) | copy-start | bytes 7684
  7.2 96.4 %all-gather.15.cloned.1.call-start = ((), (), s32[]{:S(2)}) async-start(), calls=%async_computation.4 | async-start | bytes 2113536 | tf_op jit(solution)/shard_map/all_gather | solution.py:95
  7.9 135.2 %all-gather.11.cloned.1.call-start = ((), (), s32[]{:S(2)}) async-start(), calls=%async_computation.1 | async-start | bytes 1320960 | tf_op jit(solution)/shard_map/all_gather | solution.py:98
  8.7 202.1 %all-gather.17.cloned.1.call-start = ((), (), s32[]{:S(2)}) async-start(), calls=%async_computation.5 | async-start | bytes 4227072 | tf_op jit(solution)/shard_map/all_gather | solution.py:99
  9.4 268.8 %all-gather.19.cloned.1.call-start = ((), (), s32[]{:S(2)}) async-start(), calls=%async_computation.6 | async-start | bytes 4227072 | tf_op jit(solution)/shard_map/all_gather | solution.py:100
  10.0 334.2 %all-gather.13.cloned.1.call-start = ((), (), s32[]{:S(2)}) async-start(), calls=%async_computation.2 | async-start | bytes 2641920 | tf_op jit(solution)/shard_map/all_gather | solution.py:101
  50.3 41.0 %copy-start.33 = (bf16[640,256]{1,0:T(8,128)(2,1)}, bf16[640,256]{1,0:T(8,128)(2,1)S(1)}, u32[]{:S(2)}) copy-start(bf16[640,256]{1,0:T(8,128)(2,1)S(1)} %reshape.404) | copy-start | bytes 983044
  50.4 40.7 %copy-start.2 = (bf16[256,640]{1,0:T(8,128)(2,1)S(1)}, bf16[256,640]{1,0:T(8,128)(2,1)}, u32[]{:S(2)}) copy-start(bf16[256,640]{1,0:T(8,128)(2,1)} %param.16) | copy-start | bytes 983044
  50.4 40.7 %copy-start.49 = (f32[640]{0:T(1024)S(1)}, f32[640]{0:T(1024)}, u32[]{:S(2)}) copy-start(f32[640]{0:T(1024)} %param.25) | copy-start | bytes 7684
  50.4 47.5 %copy-start.80 = (f32[128]{0:T(128)}, f32[128]{0:T(128)S(1)}, u32[]{:S(2)}) copy-start(f32[128]{0:T(128)S(1)} %negate_power_fusion) | copy-start | bytes 1540
  50.4 47.4 %copy-start.59 = (f32[256]{0:T(256)}, f32[256]{0:T(256)S(1)}, u32[]{:S(2)}) copy-start(f32[256]{0:T(256)S(1)} %get-tuple-element.70) | copy-start | bytes 3076
  53.1 41.2 %copy-start.83 = (f32[256]{0:T(256)}, f32[256]{0:T(256)S(1)}, u32[]{:S(2)}) copy-start(f32[256]{0:T(256)S(1)} %get-tuple-element.56) | copy-start | bytes 3076
  54.6 43.9 %collective-permute-start = (bf16[256,256]{0,1:T(8,128)(2,1)S(1)}, bf16[256,256]{0,1:T(8,128)(2,1)S(1)}, u32[]{:S(2)}, u32[]{:S(2)}) collective-permute-start(bf16[256,256]{0,1:T(8,128)(2,1)S(1)} %pad_maximum_fusion.6), channel_id=1, source_target_pairs={{0,1},{1,2},{2,3},{3,4},{4,5},{5,6},{6,7},{7,8},{8,9},{9,10},{10,1... | collective-permute-start | bytes 393224 | tf_op jit(solution)/shard_map/ppermute | solution.py:19
  56.8 565.6 %all-reduce.14.cloned.1.call-start = ((), (), s32[]{:S(2)}) async-start(), calls=%async_computation.7 | async-start | bytes 34078720
  91.1 3.3 copy-start.35
  91.4 6.5 copy-start.50
  91.4 9.1 collective-permute-start.2
  98.4 11.1 copy-start.37
  98.4 11.1 copy-start.38
  98.4 9.5 copy-start.86
  98.4 11.4 collective-permute-start.1
  100.5 12.3 collective-permute-start.3
  117.8 29.8 %copy-start.53 = (f32[640]{0:T(1024)S(1)}, f32[640]{0:T(1024)}, u32[]{:S(2)}) copy-start(f32[640]{0:T(1024)} %param.29) | copy-start | bytes 7684
  283.9 4.3 copy-start.7
  283.9 4.3 copy-start.12
  344.2 3.3 copy-start.20
  344.2 3.3 copy-start.58
  344.2 4.2 copy-start.4
  344.2 5.2 copy-start.85
  344.2 5.2 copy-start.91
  356.2 3.3 copy-start.8
  356.2 3.3 copy-start.66
  374.3 11.5 collective-permute-start.4
  380.0 3.6 copy-start.17
  380.0 3.6 copy-start.22
  380.0 8.0 collective-permute-start.6
  383.6 7.6 copy-start.60
  383.6 7.6 copy-start.81
  383.6 8.2 copy-start.25
  383.7 8.2 copy-start.62
  383.7 8.2 copy-start.73
  385.8 6.3 copy-start.84
  386.7 4.5 collective-permute-start.5
  388.1 5.4 collective-permute-start.7
  394.7 874.5 %reduce-scatter.2.cloned.1.call-start = ((), (), s32[]{:S(2)}) async-start(), calls=%async_computation.3 | async-start | bytes 5283840 | tf_op jit(solution)/shard_map/reduce_scatter | solution.py:218
  400.8 74.6 %copy-start.75 = (f32[256]{0:T(256)S(1)}, f32[256]{0:T(256)}, u32[]{:S(2)}) copy-start(f32[256]{0:T(256)} %copy-done.74) | copy-start | bytes 3076
  400.8 74.6 %copy-start.15 = (f32[256,640]{1,0:T(8,128)S(1)}, f32[256,640]{1,0:T(8,128)}, u32[]{:S(2)}) copy-start(f32[256,640]{1,0:T(8,128)} %copy-done.14) | copy-start | bytes 1966084
  (59 other events, 92.9 us)
Sparse Core Ops, SparseCore 0:
  11.2 67.7 all-gather.14
  81.8 61.3 all-gather.10
  146.3 64.4 all-gather.16
  213.9 64.3 all-gather.18
  281.2 62.9 all-gather.12
  394.8 227.5 all-reduce.13
  625.4 643.7 reduce-scatter.1
where the time goes:
time: 1280 us
  waiting for transfers between devices  991 us (77%)
  blocking collectives  145 us (11%)
  matrix products  48.8 us (4%)
  local copies, waits for them, and re-layouts  42.6 us (3%)
  between operations  16.5 us (1%)
  other arithmetic  16.4 us (1%)
  starting transfers between devices  16.1 us (1%)
    reduce_scatter x1, waiting for transfers between devices, body(): lax.psum_scatter(grad_down, 'seq', scatter_dimension=0, tiled=True)  638 us
    unnamed x8, waiting for transfers between devices  149 us
    psum x1, blocking collectives, body(): lax.psum((grad_input, grad_query_gain, grad_key_gain, grad_attn, grad_ffn...  72.5 us
    all_gather x1, waiting for transfers between devices, body(): lax.all_gather(gate_weight, 'seq', axis=0, tiled=True)  62.4 us
    all_gather x1, waiting for transfers between devices, body(): lax.all_gather(up_weight, 'seq', axis=0, tiled=True)  61.8 us
    all_gather x1, waiting for transfers between devices, body(): lax.all_gather(down_weight, 'seq', axis=0, tiled=True)  53.1 us
    all_gather x1, blocking collectives, body(): lax.all_gather(key_weight, 'seq', axis=0, tiled=True)  38.2 us
    all_gather x1, blocking collectives, body(): lax.all_gather(value_weight, 'seq', axis=0, tiled=True)  34 us
  transfers between devices with their start and end apart: 15, of which 7 were waited for; matrix products, arithmetic and copies ran while one was open for 5% of the time, Pallas kernels for 0%

commit v1 on v0

v1 whole, which is shorter than its diff:
```python
from functools import partial
import math

import jax
import jax.numpy as jnp
from jax import lax
from jax.sharding import Mesh, PartitionSpec as P

WINDOW = 512
ALL = ("y", "x", "z", "c")

norm_epsilon = 1e-06
rope_base = 10000.0
bf16 = jnp.bfloat16
f32 = jnp.float32


def shifted(value, steps):
    count = lax.axis_size(ALL)
    leading, last = (max(0, -steps), min(count, count - steps))
    return lax.ppermute(value, ALL, [(source, source + steps) for source in range(leading, last)])


def rms_scale(values, gain):
    mean_square = jnp.mean(values * values, axis=-1, keepdims=True)
    return values * lax.rsqrt(mean_square + norm_epsilon) * gain


def rope_tables(position, head_dim):
    half = head_dim // 2
    exponent = jnp.arange(half, dtype=jnp.float32) * (2.0 / head_dim)
    inverse = jnp.power(jnp.float32(rope_base), -exponent)
    angles = position.astype(jnp.float32)[:, None] * inverse[None, :]
    return (jnp.cos(angles)[:, None, :], jnp.sin(angles)[:, None, :])


def head_prep(pre, gain, cosine, sine):
    normed = rms_scale(pre, gain)
    half = normed.shape[-1] // 2
    first = normed[..., :half]
    second = normed[..., half:]
    return jnp.concatenate(
        [first * cosine - second * sine, second * cosine + first * sine], axis=-1
    )


def gated(gate, upward):
    return jax.nn.gelu(gate, approximate=True) * upward


def product(left, right):
    return jnp.dot(left, right, preferred_element_type=jnp.float32)


def transposed_left(left, right):
    return lax.dot_general(
        left, right, (((0,), (0,)), ((), ())), preferred_element_type=jnp.float32
    )


def transposed_right(left, right):
    return lax.dot_general(
        left, right, (((1,), (1,)), ((), ())), preferred_element_type=jnp.float32
    )


def swap_core(value):
    return lax.ppermute(value, "c", [(0, 1), (1, 0)])


def split_columns(grads):
    core = lax.axis_index("c")
    mine, theirs = [], []
    for grad in grads:
        half = grad.shape[1] // 2
        first, second = grad[:, :half], grad[:, half:]
        mine.append(jnp.where(core == 0, first, second))
        theirs.append(jnp.where(core == 0, second, first))
    mine = jnp.concatenate(mine, axis=1) if len(mine) > 1 else mine[0]
    theirs = jnp.concatenate(theirs, axis=1) if len(theirs) > 1 else theirs[0]
    other = swap_core(theirs.astype(bf16))
    return mine + other.astype(f32)


def split_rows(grads):
    core = lax.axis_index("c")
    mine, theirs = [], []
    for grad in grads:
        own = grad.shape[0] // 128
        parts = grad.reshape(16, 4, 2, own, grad.shape[1])
        first = parts[:, :, 0].reshape(16, 4 * own, grad.shape[1])
        second = parts[:, :, 1].reshape(16, 4 * own, grad.shape[1])
        mine.append(jnp.where(core == 0, first, second))
        theirs.append(jnp.where(core == 0, second, first))
    mine = jnp.concatenate(mine, axis=1)
    theirs = jnp.concatenate(theirs, axis=1)
    other = swap_core(theirs.astype(bf16))
    return mine + other.astype(f32)


def spread(value, axes):
    return lax.all_to_all(value, axes, split_axis=0, concat_axis=0, tiled=True)


def high_low(value):
    high = value.astype(bf16)
    low = (value - high.astype(f32)).astype(bf16)
    return high, low


def body(
    tokens,
    starts,
    query_weight,
    key_weight,
    value_weight,
    output_weight,
    gate_weight,
    up_weight,
    down_weight,
    input_gain,
    query_gain,
    key_gain,
    attn_gain,
    ffn_gain,
    ffn_out_gain,
    cotangent,
):
    span, width = tokens.shape
    head_dim = key_weight.shape[1]
    heads = query_weight.shape[1] // head_dim
    hq = heads * head_dim
    ff = gate_weight.shape[1]
    devices = lax.axis_size(ALL)
    hops = max(1, WINDOW // span)
    extent = hops * span + span
    scale = 1.0 / math.sqrt(head_dim)
    columns = jnp.concatenate([query_weight, key_weight, value_weight, gate_weight, up_weight], axis=1)
    rows = columns.shape[0]
    columns = jnp.pad(columns, ((0, 8 - rows), (0, 0)))
    packed = jnp.concatenate([columns, output_weight, down_weight[:8], down_weight[8:]], axis=1)
    gathered = lax.all_gather(packed, ALL, axis=0, tiled=False)
    wide = columns.shape[1]
    full_columns = gathered[:, :rows, :wide].reshape(devices * rows, wide)
    full_query = full_columns[:, :hq]
    full_key = full_columns[:, hq : hq + head_dim]
    full_value = full_columns[:, hq + head_dim : hq + 2 * head_dim]
    full_gate = full_columns[:, hq + 2 * head_dim : hq + 2 * head_dim + ff]
    full_up = full_columns[:, hq + 2 * head_dim + ff :]
    full_output = gathered[:, :, wide : wide + width].reshape(devices * 8, width)
    full_down = jnp.concatenate(
        [gathered[:, :, wide + width : wide + 2 * width], gathered[:, :, wide + 2 * width :]], axis=1
    ).reshape(devices * 16, width)

    group = lax.axis_index(ALL)
    group_ids = jnp.arange(starts.shape[0], dtype=jnp.int32)
    first_group = jnp.max(jnp.where((group_ids <= group) & (starts == 1), group_ids, 0))
    seq_first = first_group * span
    query_global = group * span + jnp.arange(span, dtype=jnp.int32)
    position = query_global - seq_first
    x_float = tokens.astype(jnp.float32)
    normed_in = rms_scale(x_float, input_gain).astype(bf16)
    query_pre = product(normed_in, full_query).reshape(span, heads, head_dim)
    key_pre = product(normed_in, full_key).reshape(span, 1, head_dim)
    value_bf = product(normed_in, full_value).astype(bf16)
    cosine, sine = rope_tables(position, head_dim)
    prepare = partial(head_prep, cosine=cosine, sine=sine)
    query_bf = prepare(query_pre, query_gain).astype(bf16)
    key_bf = prepare(key_pre, key_gain).astype(bf16).reshape(span, head_dim)
    pair = jnp.concatenate([key_bf, value_bf], axis=1)
    received = [shifted(pair, step) for step in range(hops, 0, -1)]
    both_all = jnp.concatenate(received + [pair], axis=0)
    keys_all = both_all[:, :head_dim]
    values_all = both_all[:, head_dim:]
    key_global = group * span - hops * span + jnp.arange(extent, dtype=jnp.int32)
    offset = query_global[:, None] - key_global[None, :]
    valid = (offset >= 0) & (offset < WINDOW) & (key_global[None, :] >= seq_first)
    query_flat = query_bf.reshape(span * heads, head_dim)
    scores = (transposed_right(query_flat, keys_all) * scale).reshape(span, heads, extent)
    scores = jnp.where(valid[:, None, :], scores, -1e30)
    peak = jnp.max(scores, axis=-1, keepdims=True)
    log_total = peak + jnp.log(jnp.sum(jnp.exp(scores - peak), axis=-1, keepdims=True))
    probs = jnp.exp(scores - log_total).reshape(span * heads, extent)
    probs_bf = probs.astype(bf16)
    attended_bf = product(probs_bf, values_all).reshape(span, heads * head_dim).astype(bf16)
    projected = product(attended_bf, full_output)
    resid = x_float + rms_scale(projected, attn_gain)
    normed_ffn = rms_scale(resid, ffn_gain).astype(bf16)
    gate = product(normed_ffn, full_gate)
    upward = product(normed_ffn, full_up)
    mixed_bf = gated(gate, upward).astype(bf16)
    down = product(mixed_bf, full_down)
    output = resid + rms_scale(down, ffn_out_gain)
    out_grad = cotangent.astype(jnp.float32)
    d_down, grad_ffn_out = jax.vjp(rms_scale, down, ffn_out_gain)[1](out_grad)
    d_down_bf = d_down.astype(bf16)
    grad_down = transposed_left(mixed_bf, d_down_bf)
    d_mixed = transposed_right(d_down_bf, full_down)
    d_gate, d_upward = jax.vjp(gated, gate, upward)[1](d_mixed)
    d_gate_bf = d_gate.astype(bf16)
    d_upward_bf = d_upward.astype(bf16)
    grad_gate = transposed_left(normed_ffn, d_gate_bf)
    grad_up = transposed_left(normed_ffn, d_upward_bf)
    part = split_columns([grad_gate, grad_up]).astype(bf16)
    ffn_near = jnp.sum(
        spread(part, ("y", "x")).reshape(16, -1, part.shape[1]).astype(f32), axis=0
    )
    d_normed_ffn = transposed_right(d_gate_bf, full_gate) + transposed_right(d_upward_bf, full_up)
    d_resid_part, grad_ffn = jax.vjp(rms_scale, resid, ffn_gain)[1](d_normed_ffn)
    d_resid = out_grad + d_resid_part
    d_projected, grad_attn = jax.vjp(rms_scale, projected, attn_gain)[1](d_resid)
    d_projected_bf = d_projected.astype(bf16)
    grad_output = transposed_left(attended_bf, d_projected_bf)
    part = split_rows([grad_output, grad_down]).astype(bf16)
    row_near = jnp.sum(spread(part, ("y", "x")).astype(f32), axis=0)
    d_attended_bf = transposed_right(d_projected_bf, full_output).astype(bf16)
    d_attended_bf = d_attended_bf.reshape(span * heads, head_dim)
    d_probs = transposed_right(d_attended_bf, values_all)
    balance = jnp.sum(d_probs * probs, axis=-1, keepdims=True)
    d_scores_bf = (probs * (d_probs - balance)).astype(bf16)
    d_query_bf = (
        (product(d_scores_bf, keys_all) * scale).astype(bf16).reshape(span, heads, head_dim)
    )
    d_keys_all = transposed_left(d_scores_bf, query_flat) * scale
    d_values_all = transposed_left(probs_bf, d_attended_bf)
    d_both_all = jnp.concatenate([d_keys_all, d_values_all], axis=1)
    d_both = d_both_all[hops * span :]
    for step in range(1, hops + 1):
        begin = (hops - step) * span
        d_both = d_both + shifted(d_both_all[begin : begin + span].astype(bf16), -step).astype(f32)
    d_key_bf = d_both[:, :head_dim].astype(bf16)
    d_value_bf = d_both[:, head_dim:].astype(bf16)
    d_key_pre, grad_key_gain = jax.vjp(prepare, key_pre, key_gain)[1](
        d_key_bf.astype(jnp.float32).reshape(span, 1, head_dim)
    )
    d_key_pre_bf = d_key_pre.reshape(span, head_dim).astype(bf16)
    d_query_pre, grad_query_gain = jax.vjp(prepare, query_pre, query_gain)[1](
        d_query_bf.astype(jnp.float32)
    )
    d_query_pre_bf = d_query_pre.reshape(span, heads * head_dim).astype(bf16)
    grad_query = transposed_left(normed_in, d_query_pre_bf)
    grad_key = transposed_left(normed_in, d_key_pre_bf)
    grad_value = transposed_left(normed_in, d_value_bf)
    d_normed_in = (
        transposed_right(d_query_pre_bf, full_query)
        + transposed_right(d_key_pre_bf, full_key)
        + transposed_right(d_value_bf, full_value)
    )
    d_input_part, grad_input = jax.vjp(rms_scale, x_float, input_gain)[1](d_normed_in)
    input_grad = (d_resid + d_input_part).astype(bf16)

    gains = jnp.concatenate(
        [grad_input, grad_query_gain, grad_key_gain, grad_attn, grad_ffn, grad_ffn_out]
    ).reshape(4, -1)
    part = split_columns([grad_query, grad_key, grad_value]).astype(bf16)
    part = part.reshape(16, -1, part.shape[1])
    carried = jnp.concatenate(high_low(gains), axis=0)
    part = jnp.concatenate([part, jnp.broadcast_to(carried, (16,) + carried.shape)], axis=1)
    near = jnp.sum(spread(part, ("y", "x")).astype(f32), axis=0)
    kept = near.shape[0] - 8
    gains = near[kept : kept + 4] + near[kept + 4 :]
    columns = jnp.concatenate([near[:kept], ffn_near], axis=1).astype(bf16)
    columns = jnp.pad(columns.reshape(8, rows, -1), ((0, 0), (0, 8 - rows), (0, 0)))
    carried = jnp.concatenate(high_low(gains), axis=0)
    carried = jnp.broadcast_to(carried, (8,) + carried.shape)
    own = jnp.arange(2).reshape(1, 2, 1, 1) == lax.axis_index("c")
    out_rows = row_near[: 4 * 8].reshape(4, 1, 8, width)
    down_rows = row_near[4 * 8 :].reshape(4, 1, 2, 8, width)
    row_part = jnp.concatenate([out_rows, down_rows[:, :, 0], down_rows[:, :, 1]], axis=3)
    row_part = jnp.where(own, row_part, 0.0).astype(bf16).reshape(8, 8, 3 * width)
    last = jnp.concatenate([columns, row_part, carried], axis=2)
    arrived = spread(last, ("z", "c")).astype(f32).reshape(4, 2, 8, last.shape[2]).sum(axis=0)
    near_wide = columns.shape[2]
    both = arrived[:, :rows, :near_wide]
    sizes = [hq // 2, head_dim // 2, head_dim // 2, ff // 2, ff // 2]
    column_grads, begin = [], 0
    for size in sizes:
        piece = both[:, :, begin : begin + size]
        column_grads.append(jnp.concatenate([piece[0], piece[1]], axis=1))
        begin += size
    both = arrived.sum(axis=0)
    sum_output = both[:, near_wide : near_wide + width]
    sum_down = jnp.concatenate(
        [both[:, near_wide + width : near_wide + 2 * width], both[:, near_wide + 2 * width : near_wide + 3 * width]],
        axis=0,
    )
    gains = both[:, near_wide + 3 * width :]
    gains = (gains[:4] + gains[4:]).reshape(-1)
    outs, begin = [], 0
    for size in (width, head_dim, head_dim, width, width, width):
        outs.append(gains[begin : begin + size])
        begin += size
    return (
        output.astype(bf16),
        input_grad,
        column_grads[0],
        column_grads[1],
        column_grads[2],
        sum_output,
        column_grads[3],
        column_grads[4],
        sum_down,
        *outs,
    )


def solution(mesh):
    inner = Mesh(mesh.devices.reshape(4, 4, 4, 2), ALL)
    split = P(ALL, None)
    return jax.shard_map(
        body,
        mesh=inner,
        in_specs=(split, P()) + (split,) * 7 + (P(),) * 6 + (split,),
        out_specs=(split,) * 9 + (P(),) * 6,
        check_vma=False,
    )
```

time: 1280 us -> 370 us (0.29)
  waiting for transfers between devices: 991 us -> 154 us
  blocking collectives: 145 us -> 0 us
  other arithmetic: 16.4 us -> 56.7 us
  starting transfers between devices: 16.1 us -> 34.9 us
    reduce_scatter x1 -> x0, waiting for transfers between devices: 638 us -> none  [body(): lax.psum_scatter(grad_down, 'seq', scatter_dimension=0, tiled=True)]
    unnamed x8 -> x1, waiting for transfers between devices: 149 us -> 0.02 us
    all_gather x5 -> x1, waiting for transfers between devices: 203 us -> 74.7 us  [body(): gathered = lax.all_gather(packed, ALL, axis=0, tiled=False)]
    all_to_all x0 -> x4, waiting for transfers between devices: none -> 79.4 us  [spread(): return lax.all_to_all(value, axes, split_axis=0, concat_axis=0, tiled=True)]
    psum x1 -> x0, blocking collectives: 72.5 us -> none  [body(): lax.psum((grad_input, grad_query_gain, grad_key_gain, grad_attn, grad_ffn...]
    all_gather x2 -> x0, blocking collectives: 72.2 us -> none  [the longest x1 38.2 us: body(): lax.all_gather(key_weight, 'seq', axis=0, tiled=True)]
    unnamed x196 -> x132, local copies, waits for them, and re-layouts: 33.1 us -> 10.5 us
    all_to_all x0 -> x4, starting transfers between devices: none -> 21.9 us  [spread(): return lax.all_to_all(value, axes, split_axis=0, concat_axis=0, tiled=True)]
  transfers between devices with their start and end apart: 15 -> 12, of which waited for: 7 -> 6; matrix products, arithmetic and copies ran while one was open for 5% -> 18% of each run, Pallas kernels for 0% -> 0%
where the time goes in v1:
time: 370 us; the launch traced here: 363 us
  waiting for transfers between devices  154 us (42%)
  other arithmetic  56.7 us (15%)
  local copies, waits for them, and re-layouts  52.4 us (14%)
  matrix products  48.7 us (13%)
  starting transfers between devices  34.9 us (9%)
  between operations  16.3 us (4%)
    all_to_all x4, waiting for transfers between devices, spread(): return lax.all_to_all(value, axes, split_axis=0, concat_axis=0, tiled=True)  79.4 us
    all_gather x1, waiting for transfers between devices, body(): gathered = lax.all_gather(packed, ALL, axis=0, tiled=False)  74.7 us
    all_to_all x4, starting transfers between devices, spread(): return lax.all_to_all(value, axes, split_axis=0, concat_axis=0, tiled=True)  21.9 us
    dot_general x9, matrix products, product(): return jnp.dot(left, right, preferred_element_type=jnp.float32)  17.1 us
    dot_general x9, matrix products, transposed_left(): lax.dot_general(left, right, (((0,), (0,)), ((), ())), preferred_element_...  15.9 us
    dot_general x9, matrix products, transposed_right(): lax.dot_general(left, right, (((1,), (1,)), ((), ())), preferred_element_...  15.8 us
    reshape x1, local copies, waits for them, and re-layouts, body(): full_columns = gathered[:, :rows, :wide].reshape(devices * rows, wide)  13.6 us
    unnamed x132, local copies, waits for them, and re-layouts  10.5 us
  transfers between devices with their start and end apart: 12, of which 6 were waited for; matrix products, arithmetic and copies ran while one was open for 18% of the time, Pallas kernels for 0%

profile of v1, /device:TPU:0, one launch (start us, length us, event | category | flops | bytes accessed | tf_op | source)
XLA Modules:
  0.0 363.3 jit_solution(15049494401850309647)
XLA Ops:
  16.7 1.8 copy.54
  19.2 74.7 %all-gather.3.cloned.1.call-done = bf16[1024,7552]{1,0:T(8,128)(2,1)} async-done(((bf16[8,7552]{1,0:T(8,128)(2,1)}), bf16[1024,7552]{1,0:T(8,128)(2,1)}) %all-gather.3.cloned.1.call-update) | async-done | bytes 15466512 | tf_op jit(solution)/shard_map/all_gather | solution.py:142
  93.9 9.9 %slice.285 = bf16[128,5,5632]{2,1,0:T(8,128)(2,1)} slice(bf16[128,8,7552]{2,1,0:T(8,128)(2,1)} %bitcast.125), slice={[0:128], [0:5], [0:5632]} | slice | bytes 14417920 | tf_op jit(solution)/shard_map/slice | solution.py:144
  103.9 13.6 %reshape.454 = bf16[640,5632]{1,0:T(8,128)(2,1)} reshape(bf16[128,5,5632]{2,1,0:T(8,128)(2,1)} %slice.285) | data formatting | bytes 14417920 | tf_op jit(solution)/shard_map/reshape | solution.py:144
  118.8 1.4 multiply_reduce_fusion.11
  122.4 2.9 collective-permute-start.1
  125.2 3.0 collective-permute-start
  128.2 2.9 fusion.27
  131.2 3.0 fusion.118
  134.2 1.7 reshape.455
  137.9 1.7 pad_maximum_fusion
  142.5 1.5 convolution_convert_fusion.1
  144.0 2.2 convert_element_type.164
  146.2 2.1 multiply_reduce_fusion.10
  148.8 2.9 fusion.9
  151.7 3.2 multiply_convert_fusion.2
  157.4 2.5 fusion.17
  164.5 2.7 convolution_convert_fusion
  167.2 2.2 reshape.458
  169.4 1.9 multiply_reduce_fusion
  176.1 3.3 fusion.127
  179.4 3.2 fusion.126
  182.6 3.3 fusion.125
  188.1 1.6 collective-permute-start.2
  193.4 2.1 fusion.112
  196.5 1.9 fusion.63
  198.5 1.4 slice_select_fusion.3
  199.9 3.1 select_convert_fusion
  203.2 1.5 pad_maximum_fusion.2
  204.7 1.8 collective-permute-start.6
  207.0 1.7 pad_maximum_fusion.1
  214.3 2.2 convolution_add_fusion
  216.5 2.2 fusion.39
  223.5 1.5 fusion.18
  226.2 10.5 %all-to-all-start = ((bf16[16,48,768]{2,1,0:T(8,128)(2,1)}), bf16[16,48,768]{2,1,0:T(8,128)(2,1)}, u32[]{:S(2)}, u32[]{:S(2)}) async-start(bf16[16,48,768]{2,1,0:T(8,128)(2,1)} %pad_maximum_fusion.4), calls=%async_computation | async-start | bytes 2359296 | tf_op jit(solution)/shard_map/all_to_all | solution.py:102
  236.8 3.0 slice_select_fusion
  239.8 3.4 fusion.1
  243.2 13.2 %all-to-all-done = bf16[16,48,768]{2,1,0:T(8,128)(2,1)} async-done(((bf16[16,48,768]{2,1,0:T(8,128)(2,1)}), bf16[16,48,768]{2,1,0:T(8,128)(2,1)}, u32[]{:S(2)}, u32[]{:S(2)}) %all-to-all-start) | async-done | bytes 1179680 | tf_op jit(solution)/shard_map/all_to_all | solution.py:102
  256.4 4.1 %all-to-all-start.2 = ((bf16[16,96,640]{2,1,0:T(8,128)(2,1)}), bf16[16,96,640]{2,1,0:T(8,128)(2,1)S(1)}, u32[]{:S(2)}, u32[]{:S(2)}) async-start(bf16[16,96,640]{2,1,0:T(8,128)(2,1)} %fusion.1), calls=%async_computation.2 | async-start | bytes 3932160 | tf_op jit(solution)/shard_map/all_to_all | solution.py:102
  260.5 3.2 slice_select_fusion.1
  265.0 4.2 %fusion = bf16[640,2048]{1,0:T(8,128)(2,1)} fusion(f32[640,1024]{1,0:T(8,128)S(1)} %slice_select_fusion.1, f32[640,1024]{1,0:T(8,128)S(1)} %slice_select_fusion.2, bf16[640,2048]{1,0:T(8,128)(2,1)} %collective-permute-done.5), kind=kLoop, calls=%fused_computation.1 | loop fusion | flops 5242880 | bytes 10485760 | tf_op jit(solution)/shard_map/convert_element_type | solution.py:204
  269.2 20.3 %all-to-all-done.2 = bf16[16,96,640]{2,1,0:T(8,128)(2,1)S(1)} async-done(((bf16[16,96,640]{2,1,0:T(8,128)(2,1)}), bf16[16,96,640]{2,1,0:T(8,128)(2,1)S(1)}, u32[]{:S(2)}, u32[]{:S(2)}) %all-to-all-start.2) | async-done | bytes 1966112 | tf_op jit(solution)/shard_map/all_to_all | solution.py:102
  290.9 3.7 %all-to-all-start.1 = ((bf16[16,40,2048]{2,1,0:T(8,128)(2,1)}), bf16[16,40,2048]{2,1,0:T(8,128)(2,1)S(1)}, u32[]{:S(2)}, u32[]{:S(2)}) async-start(bf16[16,40,2048]{2,1,0:T(8,128)(2,1)} %bitcast.15), calls=%async_computation.1 | async-start | bytes 5242880 | tf_op jit(solution)/shard_map/all_to_all | solution.py:102
  294.7 1.4 convert_reduce_fusion.1
  296.3 1.8 convert_reduce_fusion
  298.2 34.7 %all-to-all-done.1 = bf16[16,40,2048]{2,1,0:T(8,128)(2,1)S(1)} async-done(((bf16[16,40,2048]{2,1,0:T(8,128)(2,1)}), bf16[16,40,2048]{2,1,0:T(8,128)(2,1)S(1)}, u32[]{:S(2)}, u32[]{:S(2)}) %all-to-all-start.1) | async-done | bytes 2621472 | tf_op jit(solution)/shard_map/all_to_all | solution.py:102
  334.6 3.5 all-to-all-start.3
  339.1 11.2 %all-to-all-done.3 = bf16[8,8,5504]{2,1,0:T(8,128)(2,1)S(1)} async-done(((bf16[8,8,5504]{2,1,0:T(8,128)(2,1)}), bf16[8,8,5504]{2,1,0:T(8,128)(2,1)S(1)}, u32[]{:S(2)}, u32[]{:S(2)}) %all-to-all-start.3) | async-done | bytes 704544 | tf_op jit(solution)/shard_map/all_to_all | solution.py:102
  (268 shorter events, 60.1 us)
Async XLA Ops:
  7.2 86.7 %all-gather.3.cloned.1.call-start = ((), (), s32[]{:S(2)}) async-start(), calls=%async_computation.4 | async-start | bytes 15587328 | tf_op jit(solution)/shard_map/all_gather | solution.py:142
  15.3 3.3 copy-start.3
  19.2 120.4 %copy-start.35 = (f32[256,128]{1,0:T(8,128)}, f32[256,128]{1,0:T(8,128)S(1)}, u32[]{:S(2)}) copy-start(f32[256,128]{1,0:T(8,128)S(1)} %get-tuple-element.73) | copy-start | bytes 393220
  19.2 120.4 %copy-start.36 = (f32[256,128]{1,0:T(8,128)}, f32[256,128]{1,0:T(8,128)S(1)}, u32[]{:S(2)}) copy-start(f32[256,128]{1,0:T(8,128)S(1)} %get-tuple-element.74) | copy-start | bytes 393220
  103.9 13.6 %copy-start.47 = (f32[640]{0:T(1024)S(1)}, f32[640]{0:T(1024)}, u32[]{:S(2)}) copy-start(f32[640]{0:T(1024)} %param.25) | copy-start | bytes 7684
  117.4 3.5 copy-start.52
  118.8 2.8 copy-start.45
  122.4 17.6 %collective-permute-start.1 = (bf16[256,512]{0,1:T(8,128)(2,1)}, bf16[256,512]{0,1:T(8,128)(2,1)}, u32[]{:S(2)}, u32[]{:S(2)}) collective-permute-start(bf16[256,512]{0,1:T(8,128)(2,1)} %pad_maximum_fusion.10), channel_id=1, source_target_pairs={{0,1},{1,2},{2,3},{3,4},{4,5},{5,6},{6,7},{7,8},{8,9},{9,10},{10,1... | collective-permute-start | bytes 786440 | tf_op jit(solution)/shard_map/ppermute | solution.py:21
  125.2 14.7 %collective-permute-start = (bf16[256,512]{0,1:T(8,128)(2,1)}, bf16[256,512]{0,1:T(8,128)(2,1)}, u32[]{:S(2)}, u32[]{:S(2)}) collective-permute-start(bf16[256,512]{0,1:T(8,128)(2,1)} %pad_maximum_fusion.10), channel_id=1, source_target_pairs={{0,2},{1,3},{2,4},{3,5},{4,6},{5,7},{6,8},{7,9},{8,10},{9,11},{10,... | collective-permute-start | bytes 786440 | tf_op jit(solution)/shard_map/ppermute | solution.py:21
  134.2 2.3 copy-start.51
  135.9 3.7 %copy-start = (f32[256,4,256]{2,1,0:T(4,128)}, f32[256,4,256]{2,1,0:T(4,128)S(1)}, u32[]{:S(2)}) copy-start(f32[256,4,256]{2,1,0:T(4,128)S(1)} %reshape.455) | copy-start | bytes 3145732
  136.5 3.1 copy-start.29
  139.9 2.1 copy-start.37
  144.0 4.3 %copy-start.48 = (f32[640]{0:T(1024)S(1)}, f32[640]{0:T(1024)}, u32[]{:S(2)}) copy-start(f32[640]{0:T(1024)} %param.28) | copy-start | bytes 7684
  146.2 2.5 copy-start.50
  148.8 2.9 copy-start.9
  151.7 3.2 copy-start.25
  156.4 3.6 slice-start.6
  157.4 2.5 copy-start.32
  157.4 2.6 slice-start.7
  172.1 13.8 %copy-start.5 = (f32[768,256]{0,1:T(8,128)}, f32[768,256]{0,1:T(8,128)S(1)}, u32[]{:S(2)}) copy-start(f32[768,256]{0,1:T(8,128)S(1)} %fusion.54) | copy-start | bytes 2359300
  174.5 11.4 %copy-start.18 = (f32[768,256]{0,1:T(8,128)}, f32[768,256]{0,1:T(8,128)S(1)}, u32[]{:S(2)}) copy-start(f32[768,256]{0,1:T(8,128)S(1)} %convolution_multiply_fusion.1) | copy-start | bytes 2359300
  176.1 3.3 copy-start.10
  176.1 3.3 copy-start.44
  179.4 3.2 copy-start.42
  186.8 23.3 %collective-permute-start.3 = (bf16[256,512]{0,1:T(8,128)(2,1)}, bf16[256,512]{0,1:T(8,128)(2,1)}, u32[]{:S(2)}, u32[]{:S(2)}) collective-permute-start(bf16[256,512]{0,1:T(8,128)(2,1)} %get-tuple-element.43), channel_id=1, source_target_pairs={{2,0},{3,1},{4,2},{5,3},{6,4},{7,5},{8,6},{9,7},{10,8},{11,9},{12,... | collective-permute-start | bytes 786440 | tf_op jit(solution)/shard_map/ppermute | solution.py:21
  188.1 3.3 copy-start.1
  188.1 22.0 %collective-permute-start.2 = (bf16[256,512]{0,1:T(8,128)(2,1)}, bf16[256,512]{0,1:T(8,128)(2,1)}, u32[]{:S(2)}, u32[]{:S(2)}) collective-permute-start(bf16[256,512]{0,1:T(8,128)(2,1)} %get-tuple-element.42), channel_id=1, source_target_pairs={{1,0},{2,1},{3,2},{4,3},{5,4},{6,5},{7,6},{8,7},{9,8},{10,9},{11,1... | collective-permute-start | bytes 786440 | tf_op jit(solution)/shard_map/ppermute | solution.py:21
  193.3 2.2 copy-start.28
  198.5 8.0 %slice-start.4 = ((s8[5242880]{0:T(1024)(128)(4,1)}), s8[4194304]{0:T(1024)(128)(4,1)S(1)}, s32[]{:S(2)}) async-start(s8[5242880]{0:T(1024)(128)(4,1)} %bitcast.121), calls=%async_computation.9 | async-start | bytes 8388608
  199.9 6.6 %slice-start.5 = ((s8[5242880]{0:T(1024)(128)(4,1)}), s8[1048576]{0:T(1024)(128)(4,1)S(1)}, s32[]{:S(2)}) async-start(s8[5242880]{0:T(1024)(128)(4,1)} %bitcast.121), calls=%async_computation.10 | async-start | bytes 2097152
  203.0 3.7 %slice-start = ((s8[5242880]{0:T(1024)(128)(4,1)}), s8[4194304]{0:T(1024)(128)(4,1)S(1)}, s32[]{:S(2)}) async-start(s8[5242880]{0:T(1024)(128)(4,1)} %bitcast.117), calls=%async_computation.5 | async-start | bytes 8388608
  203.2 3.5 slice-start.1
  204.7 35.1 %collective-permute-start.6 = (bf16[16,96,640]{2,1,0:T(8,128)(2,1)}, bf16[16,96,640]{2,1,0:T(8,128)(2,1)}, u32[]{:S(2)}, u32[]{:S(2)}) collective-permute-start(bf16[16,96,640]{2,1,0:T(8,128)(2,1)} %pad_maximum_fusion.2), channel_id=1, source_target_pairs={{0,1},{1,0},{2,3},{3,2},{4,5},{5,4},{6,7},{7,6},{8,9},{9,8},{10,11... | collective-permute-start | bytes 5898248 | tf_op jit(solution)/shard_map/ppermute | solution.py:68
  208.7 56.3 %collective-permute-start.5 = (bf16[640,2048]{1,0:T(8,128)(2,1)}, bf16[640,2048]{1,0:T(8,128)(2,1)}, u32[]{:S(2)}, u32[]{:S(2)}) collective-permute-start(bf16[640,2048]{1,0:T(8,128)(2,1)} %pad_maximum_fusion.1), channel_id=1, source_target_pairs={{0,1},{1,0},{2,3},{3,2},{4,5},{5,4},{6,7},{7,6},{8,9},{9,8},{10,11... | collective-permute-start | bytes 7864328 | tf_op jit(solution)/shard_map/ppermute | solution.py:68
  210.1 2.2 copy-start.27
  211.7 7.0 %copy-start.16 = (f32[640,256]{1,0:T(8,128)}, f32[640,256]{1,0:T(8,128)S(1)}, u32[]{:S(2)}) copy-start(f32[640,256]{1,0:T(8,128)S(1)} %fusion.94) | copy-start | bytes 1966084
  214.3 4.4 %copy-start.17 = (f32[640,256]{1,0:T(8,128)}, f32[640,256]{1,0:T(8,128)S(1)}, u32[]{:S(2)}) copy-start(f32[640,256]{1,0:T(8,128)S(1)} %fusion.110) | copy-start | bytes 1966084
  219.8 3.7 %collective-permute-start.4 = (bf16[640,768]{1,0:T(8,128)(2,1)}, bf16[640,768]{1,0:T(8,128)(2,1)}, u32[]{:S(2)}, u32[]{:S(2)}) collective-permute-start(bf16[640,768]{1,0:T(8,128)(2,1)} %pad_maximum_fusion.5), channel_id=1, source_target_pairs={{0,1},{1,0},{2,3},{3,2},{4,5},{5,4},{6,7},{7,6},{8,9},{9,8},{10,11... | collective-permute-start | bytes 2949128 | tf_op jit(solution)/shard_map/ppermute | solution.py:68
  221.1 2.5 copy-start.14
  226.2 30.2 %all-to-all-start = ((bf16[16,48,768]{2,1,0:T(8,128)(2,1)}), bf16[16,48,768]{2,1,0:T(8,128)(2,1)}, u32[]{:S(2)}, u32[]{:S(2)}) async-start(bf16[16,48,768]{2,1,0:T(8,128)(2,1)} %pad_maximum_fusion.4), calls=%async_computation | async-start | bytes 2359296 | tf_op jit(solution)/shard_map/all_to_all | solution.py:102
  256.4 7.4 %slice-start.2 = ((s8[5242880]{0:T(1024)(128)(4,1)}), s8[1048576]{0:T(1024)(128)(4,1)S(1)}, s32[]{:S(2)}) async-start(s8[5242880]{0:T(1024)(128)(4,1)} %bitcast.119), calls=%async_computation.7 | async-start | bytes 2097152
  256.4 33.1 %all-to-all-start.2 = ((bf16[16,96,640]{2,1,0:T(8,128)(2,1)}), bf16[16,96,640]{2,1,0:T(8,128)(2,1)S(1)}, u32[]{:S(2)}, u32[]{:S(2)}) async-start(bf16[16,96,640]{2,1,0:T(8,128)(2,1)} %fusion.1), calls=%async_computation.2 | async-start | bytes 3932160 | tf_op jit(solution)/shard_map/all_to_all | solution.py:102
  260.5 3.8 %slice-start.3 = ((s8[5242880]{0:T(1024)(128)(4,1)}), s8[4194304]{0:T(1024)(128)(4,1)S(1)}, s32[]{:S(2)}) async-start(s8[5242880]{0:T(1024)(128)(4,1)} %bitcast.119), calls=%async_computation.8 | async-start | bytes 8388608
  290.9 42.1 %all-to-all-start.1 = ((bf16[16,40,2048]{2,1,0:T(8,128)(2,1)}), bf16[16,40,2048]{2,1,0:T(8,128)(2,1)S(1)}, u32[]{:S(2)}, u32[]{:S(2)}) async-start(bf16[16,40,2048]{2,1,0:T(8,128)(2,1)} %bitcast.15), calls=%async_computation.1 | async-start | bytes 5242880 | tf_op jit(solution)/shard_map/all_to_all | solution.py:102
  333.5 4.7 %copy-start.12 = (f32[256,640]{1,0:T(8,128)S(1)}, f32[256,640]{1,0:T(8,128)}, u32[]{:S(2)}) copy-start(f32[256,640]{1,0:T(8,128)} %copy-done.11) | copy-start | bytes 1966084
  333.5 4.7 %copy-start.24 = (f32[256,640]{1,0:T(8,128)S(1)}, f32[256,640]{1,0:T(8,128)}, u32[]{:S(2)}) copy-start(f32[256,640]{1,0:T(8,128)} %get-tuple-element.88) | copy-start | bytes 1966084
  334.6 15.7 %all-to-all-start.3 = ((bf16[8,8,5504]{2,1,0:T(8,128)(2,1)}), bf16[8,8,5504]{2,1,0:T(8,128)(2,1)S(1)}, u32[]{:S(2)}, u32[]{:S(2)}) async-start(bf16[8,8,5504]{2,1,0:T(8,128)(2,1)} %pad_maximum_fusion.6), calls=%async_computation.3 | async-start | bytes 1409024 | tf_op jit(solution)/shard_map/all_to_all | solution.py:102
  (25 other events, 34.0 us)
Sparse Core Ops, SparseCore 0:
  13.1 80.7 all-gather.2
